TPU v7x, 32 devices: a whole 2x2x4 slice. The times are simulated.
32 devices in a mesh: member: 4 (over x, core), lat: 8 (over z, y).
Axes of the slice: x: 2, y: 2, z: 4, core: 2. Of those that a mesh axis runs over, the one named last changes fastest.
Arguments:
- tokens: bfloat16 [8, 16, 360, 1024], P('member', 'lat'), may hold values from -6 to 6
- weight: bfloat16 [1024, 1328], replicated, may hold values from -0.125 to 0.125
- channels: int32 [8], replicated, may hold values from 0 to 82, as said below
- band_rows: int32 [16], P('lat'), may hold values from 0 to 179
- target: float32 [8, 64, 1440], P(None, 'lat'), may hold values from -6 to 6
Outputs:
- energy: float32 [], replicated
- grad_tokens: bfloat16 [8, 16, 360, 1024], P('member', 'lat')
- grad_weight: float32 [1024, 128], P(('member', 'lat'))
Inputs may be any that keep to these rules, and one draw needn't show every extreme that they name: `channels`: 8 different channel numbers.
All inputs are finite; a program needn't handle non-finite values.
Results may differ from a plain program's by a relative error of at most 0.0055.
Values may be sent and summed in bfloat16 or wider, within the bound.
A program may use at most 64 MiB of HBM per device.

v0:
```python
import math

import jax
import jax.numpy as jnp
from jax import lax
from jax.sharding import PartitionSpec as P

SEL = 8
P_SIZE = 4


EPSILON = 0.0001


def latitude_weights(band_rows, patch_side):
    pixel = (
        band_rows[:, None].astype(jnp.float32) * patch_side
        + jnp.arange(patch_side, dtype=jnp.float32)[None, :]
        + 0.5
    )
    return jnp.cos((90.0 - 0.25 * pixel) * (math.pi / 180.0))


def coefficients(gram_sums, members, loss_scale):
    diagonal = jnp.diagonal(gram_sums, axis1=1, axis2=2)
    squared_gap = diagonal[:, :, None] + diagonal[:, None, :] - 2.0 * gram_sums
    distance = jnp.sqrt(jnp.abs(squared_gap) + EPSILON)
    inverse = jnp.sign(squared_gap) / distance
    count_float = float(members)
    energy = jnp.sum(distance[:, :members, members]) / count_float - jnp.sum(
        distance[:, :members, :members]
    ) / (2.0 * count_float * count_float)
    pair_terms = inverse[:, :members, :members] / (count_float * count_float)
    own_terms = inverse[:, :members, members] / count_float
    diagonal_add = own_terms - jnp.sum(pair_terms, axis=2)
    member_coef = pair_terms + diagonal_add[:, :, None] * jnp.eye(members, dtype=jnp.float32)[None]
    coef = jnp.concatenate([member_coef, -own_terms[:, :, None]], axis=2) * loss_scale
    return (energy, coef)


def stack_fields(member_fields, aligned_target):
    count_all, slice_rows, _ = member_fields.shape
    shaped = member_fields.astype(jnp.float32).reshape(count_all, slice_rows, SEL, P_SIZE * P_SIZE)
    return jnp.concatenate([shaped, aligned_target[None]], axis=0)


def weighted_gram(stacked, slice_weight):
    return jnp.einsum(
        "atsp,btsp->sab",
        stacked * slice_weight[None, :, None, :],
        stacked,
        precision=lax.Precision.HIGHEST,
    )


def shards(tokens, weight, channels, band_rows, target):
    local_members, band_count, column_count, width = tokens.shape
    pixels = P_SIZE * P_SIZE
    groups = lax.axis_size("member")
    members = local_members * groups
    latitude_total = band_count * lax.axis_size("lat") * P_SIZE
    longitude_total = column_count * P_SIZE
    loss_scale = float(members * latitude_total * longitude_total)
    columns = (channels[:, None] * pixels + jnp.arange(pixels, dtype=jnp.int32)[None, :]).reshape(
        -1
    )
    head_weight = jnp.take(weight, columns, axis=1)
    token_rows = band_count * column_count
    flat_tokens = tokens.reshape(local_members * token_rows, width)
    prediction = jnp.dot(flat_tokens, head_weight, preferred_element_type=jnp.float32).astype(
        jnp.bfloat16
    )
    field = prediction.reshape(local_members, token_rows, SEL * pixels)
    row_weight = latitude_weights(band_rows, P_SIZE)
    cell_weight = jnp.broadcast_to(
        row_weight[:, None, :, None], (band_count, column_count, P_SIZE, P_SIZE)
    ).reshape(token_rows, pixels)
    aligned = (
        target.reshape(SEL, band_count, P_SIZE, column_count, P_SIZE)
        .transpose(1, 3, 0, 2, 4)
        .reshape(token_rows, SEL, pixels)
    )
    gathered = lax.all_gather(field, "member", axis=0, tiled=True)
    stacked = stack_fields(gathered, aligned)
    partial_gram = weighted_gram(stacked, cell_weight)
    gram_total, weight_sum = lax.psum((partial_gram, jnp.sum(cell_weight) * 1.0), "lat")
    energy, coef = coefficients(gram_total / weight_sum, members, loss_scale)
    own_coef = lax.dynamic_slice_in_dim(
        coef, lax.axis_index("member") * local_members, local_members, 1
    )
    combined = jnp.einsum("smb,btsp->mtsp", own_coef, stacked, precision=lax.Precision.HIGHEST)
    returned = (
        (combined * (cell_weight / weight_sum)[None, :, None, :])
        .astype(jnp.bfloat16)
        .reshape(local_members, token_rows, SEL * pixels)
    )
    upstream = returned.reshape(local_members * token_rows, SEL * pixels)
    grad_flat = lax.dot_general(
        upstream, head_weight, (((1,), (1,)), ((), ())), preferred_element_type=jnp.float32
    ).astype(jnp.bfloat16)
    grad_tokens = grad_flat.reshape(tokens.shape)
    summed = lax.psum_scatter(
        lax.dot_general(
            flat_tokens, upstream, (((0,), (0,)), ((), ())), preferred_element_type=jnp.float32
        ),
        ("member", "lat"),
        scatter_dimension=0,
        tiled=True,
    )
    token_total = members * band_count * lax.axis_size("lat") * column_count
    grad_weight = summed * (1.0 / math.sqrt(float(token_total)))
    return (energy, grad_tokens, grad_weight)


def solution(mesh):
    placed = (P("member", "lat", None, None), P(), P(), P("lat"), P(None, "lat", None))
    return jax.shard_map(
        shards,
        mesh=mesh,
        in_specs=placed,
        out_specs=(P(), P("member", "lat", None, None), P(("member", "lat"), None)),
        check_vma=False,
    )
```

profile of v0, /device:TPU:0, one launch (start us, length us, event | category | flops | bytes accessed | tf_op | source)
XLA Modules:
  0.0 248.6 jit_solution(6182757994541024352)
XLA Ops:
  7.2 0.8 broadcast_multiply_fusion.1
  8.3 3.2 %gather_fusion = bf16[128,1024]{1,0:T(8,128)(2,1)S(1)} fusion(bf16[1024,1328]{0,1:T(8,128)(2,1)} %param.6, s32[1024]{0:T(1024)S(1)} %pad_clamp_fusion), kind=kCustom, calls=%fused_computation | custom fusion | bytes 524800 | tf_op jit(solution)/shard_map/jit(_take)/gather | solution.py:67
  11.5 1.7 convolution_convert_fusion.1
  13.3 4.7 %copy.24 = f32[8,8,1440]{0,2,1:T(8,128)} copy(f32[8,8,1440]{2,1,0:T(8,128)} %param.9) | data formatting | bytes 737280 | tf_op args[4]
  18.0 5.1 %copy.25 = f32[2,360,8,4,4]{1,0,4,3,2:T(2,128)S(1)} copy(f32[2,360,8,4,4]{2,4,1,3,0:T(4,128)} %bitcast.40) | data formatting | bytes 737280 | tf_op jit(solution)/shard_map/transpose | solution.py:80
  23.1 1.5 broadcast_in_dim_reshape.4
  24.6 0.1 broadcast_in_dim.18
  24.7 0.1 mul.81
  24.8 0.7 broadcast_reduce_fusion
  25.6 9.7 %all-gather.2.cloned.1.call-done = bf16[8,720,128]{2,1,0:T(8,128)(2,1)} async-done(((bf16[2,720,128]{2,1,0:T(8,128)(2,1)}), bf16[8,720,128]{2,1,0:T(8,128)(2,1)}) %all-gather.2.cloned.1.call-update) | async-done | bytes 1474576 | tf_op jit(solution)/shard_map/all_gather | solution.py:83
  35.2 3.2 %copy.23 = f32[8,720,128]{1,0,2:T(8,128)} copy(bf16[8,720,128]{2,1,0:T(8,128)(2,1)} %all-gather.2.cloned.1.call-done) | data formatting | bytes 4423680 | tf_op jit(solution)/shard_map/reshape | solution.py:43
  38.4 13.0 %fusion.7 = f32[8,9,9]{2,1,0:T(8,128)} fusion(f32[1,720,8,16]{1,0,3,2:T(1,128)S(1)} %copy-done.2, f32[8,720,8,16]{1,0,3,2:T(8,128)} %bitcast.41, f32[720,16]{0,1:T(8,128)S(1)} %mul.81), kind=kOutput, calls=%fused_computation.13 | convolution fusion | flops 92067840 | bytes 3366432 | tf_op jit(solution)/shard_map/atsp,btsp->sab/dot_general | solution.py:48
  51.4 39.0 %all-reduce = (f32[8,9,9]{2,1,0:T(8,128)S(1)}, f32[]{:T(128)}) all-reduce(f32[8,9,9]{2,1,0:T(8,128)} %fusion.7, f32[]{:T(128)} %broadcast_reduce_fusion), channel_id=1, replica_groups=mesh['member'=4,'lat'=8] {'lat'}, use_global_device_ids=true, to_apply=%region_0.1 | all-reduce | flops 649 | bytes 5192 | tf_op jit(solution)/shard_map/psum | solution.py:86
  90.4 1.3 broadcast_divide_fusion.1
  91.7 0.7 broadcast_divide_fusion
  92.3 0.8 copy.26
  93.1 1.5 gather_fusion.1
  94.6 0.1 copy.27
  94.7 0.8 sign_divide_fusion
  95.5 0.1 fusion.10
  95.5 0.1 copy.29
  95.7 0.2 fusion.11
  95.8 0.6 slice_reduce_fusion
  96.4 7.6 %fusion.6 = bf16[2,720,8,16]{1,0,3,2:T(2,128)(2,1)} fusion(f32[1,720,8,16]{1,0,3,2:T(1,128)S(1)} %copy-done.2, f32[8,720,8,16]{1,0,3,2:T(8,128)} %bitcast.42, f32[720,16]{0,1:T(8,128)} %broadcast_divide_fusion.1, s32[]{:T(128)S(6)} %select_n.30, f32[8,8,8]{2,1,0:T(8,128)S(1)} %get-tuple-element.19, f32[8,8,1]{2,1,0:T(8,128)S(1)} %get-tuple-element.16), kind=kOutput, calls=%fused_computation.12 | convolution fusion | flops 21104928 | bytes 3734788 | tf_op jit(solution)/shard_map/smb,btsp->mtsp/dot_general | solution.py:91
  104.1 1.3 reshape_reshape.3
  105.4 1.4 convolution_bitcast_fusion
  106.8 2.0 copy.33
  108.8 0.7 slice_reduce_fusion.1
  110.8 3.5 %convolution_convert_fusion = bf16[1440,1024]{1,0:T(8,128)(2,1)} fusion(bf16[1440,128]{0,1:T(8,128)(2,1)S(1)} %reshape_reshape.3, bf16[128,1024]{1,0:T(8,128)(2,1)} %copy-done.1, pred[128]{0:T(512)(128)(4,1)S(1)} %compare_and_fusion), kind=kOutput, calls=%fused_computation.6 | convolution fusion | flops 379092992 | bytes 3580032 | tf_op jit(solution)/shard_map/dot_general | solution.py:98
  114.3 124.8 %reduce-scatter.4.cloned.1.call-done = f32[32,128]{1,0:T(8,128)} async-done(((f32[1024,128]{1,0:T(8,128)}), f32[32,128]{1,0:T(8,128)}) %reduce-scatter.4.cloned.1.call-update) | async-done | bytes 16400
  239.2 0.8 copy.34
  240.0 0.7 copy.30
  (23 shorter events, 0.5 us)
Async XLA Ops:
  7.2 4.3 %copy-start = (bf16[2,2,360,1024]{3,2,1,0:T(8,128)(2,1)S(1)}, bf16[2,2,360,1024]{3,2,1,0:T(8,128)(2,1)}, u32[]{:S(2)}) copy-start(bf16[2,2,360,1024]{3,2,1,0:T(8,128)(2,1)} %param.5) | copy-start | bytes 8847364
  7.2 28.0 %all-gather.2.cloned.1.call-start = ((), (), s32[]{:S(2)}) async-start(), calls=%async_computation.1 | async-start | bytes 1843200 | tf_op jit(solution)/shard_map/all_gather | solution.py:83
  11.5 6.5 %copy-start.1 = (bf16[128,1024]{1,0:T(8,128)(2,1)}, bf16[128,1024]{1,0:T(8,128)(2,1)S(1)}, u32[]{:S(2)}) copy-start(bf16[128,1024]{1,0:T(8,128)(2,1)S(1)} %gather_fusion) | copy-start | bytes 786436
  13.3 225.9 %reduce-scatter.4.cloned.1.call-start = ((), (), s32[]{:S(2)}) async-start(), calls=%async_computation.2 | async-start | bytes 540672
  18.0 6.6 %copy-start.3 = (s32[2]{0:T(128)S(1)}, s32[2]{0:T(128)}, u32[]{:S(2)}) copy-start(s32[2]{0:T(128)} %param.8) | copy-start | bytes 28
  24.6 13.8 %copy-start.2 = (f32[1,720,8,16]{1,0,3,2:T(1,128)S(1)}, f32[1,720,8,16]{1,0,3,2:T(1,128)}, u32[]{:S(2)}) copy-start(f32[1,720,8,16]{1,0,3,2:T(1,128)} %broadcast_in_dim_reshape.4) | copy-start | bytes 1105924
Sparse Core Ops, SparseCore 0:
  13.4 21.7 all-gather.1
  108.9 130.1 reduce-scatter.3
where the time goes:
time: 249 us
  waiting for transfers between devices  134 us (54%)
  blocking collectives  39 us (16%)
  matrix products  27.3 us (11%)
  local copies, waits for them, and re-layouts  25.3 us (10%)
  between operations  16.6 us (7%)
  other arithmetic  5.91 us (2%)
    unnamed x3, waiting for transfers between devices  125 us
    psum x1, blocking collectives, shards(): lax.psum((partial_gram, jnp.sum(cell_weight) * 1.0), 'lat')  39 us
    dot_general x1, matrix products, weighted_gram(): jnp.einsum('atsp,btsp->sab', stacked * slice_weight[None, :, None, :], st...  13 us
    all_gather x1, waiting for transfers between devices, shards(): gathered = lax.all_gather(field, 'member', axis=0, tiled=True)  9.65 us
    unnamed x12, local copies, waits for them, and re-layouts  8.23 us
    dot_general x1, matrix products, shards(): jnp.einsum('smb,btsp->mtsp', own_coef, stacked, precision=lax.Precision.H...  7.61 us
    transpose x1, local copies, waits for them, and re-layouts, shards(): aligned = target.reshape(SEL, band_count, P_SIZE, column_count, P_SIZE).t...  5.06 us
  transfers between devices with their start and end apart: 2, of which 2 were waited for; matrix products, arithmetic and copies ran while one was open for 7% of the time, Pallas kernels for 0%

commit v1 on v0

v1 whole, which is shorter than its diff:
```python
import functools
import math

import jax
import jax.numpy as jnp
from jax import lax
from jax.experimental import pallas as pl
from jax.experimental.pallas import tpu as pltpu
from jax.sharding import PartitionSpec as P

SEL = 8
P_SIZE = 4
PIX = P_SIZE * P_SIZE
LANES = SEL * PIX
EPSILON = 0.0001
F32 = jnp.float32
BF16 = jnp.bfloat16
HIGH = lax.Precision.HIGHEST
VMEM_LIMIT = 40 * 1024 * 1024


def round_up(value, step):
    return -(-value // step) * step


def iota(shape, axis):
    return lax.broadcasted_iota(jnp.int32, shape, axis)


def body(
    G,
    L,
    LM,
    BANDS,
    COLS,
    chan_ref,
    band_ref,
    tok_hbm,
    w_hbm,
    tgt_hbm,
    energy_ref,
    gtok_hbm,
    gw_ref,
    tok,
    wfull,
    head,
    head_t,
    tgt,
    wide,
    yal,
    wq,
    fields,
    rsum,
    msg,
    abuf,
    bbuf,
    crow,
    up,
    up_t,
    gout,
    s1,
    r1,
    own,
    s2,
    r2,
    ld_sem,
    p1_s,
    p1_r,
    x_s,
    x_r,
    i_s,
    i_r,
    ii_s,
    ii_r,
    iii_s,
    iii_r,
    a_s,
    a_r,
    b_s,
    b_r,
    r1_s,
    r1_r,
    r2_s,
    r2_r,
    out_s,
):
    X = G // 2
    M = G * LM
    ROWS = BANDS * COLS
    RP = fields.shape[1]
    CH = RP // G
    D = tok.shape[2]
    NBP = round_up(M + 1, 8)
    NL = M * NBP
    DB = D // G
    SB = DB // L
    me = lax.axis_index("member")
    lat = lax.axis_index("lat")
    xc = me // 2
    core = me % 2
    mate = me + 1 - 2 * core

    def dev(kind, index):
        return {kind: index}

    def remote(src, dst, ssem, rsem, kind, index):
        return pltpu.make_async_remote_copy(
            src_ref=src,
            dst_ref=dst,
            send_sem=ssem,
            recv_sem=rsem,
            device_id=dev(kind, index),
            device_id_type=pl.DeviceIdType.MESH,
        )

    w_copy = pltpu.make_async_copy(w_hbm, wfull, ld_sem.at[0])
    w_copy.start()
    t_copies = []
    for lm in range(LM):
        c = pltpu.make_async_copy(
            tok_hbm.at[lm], tok.at[lm, pl.ds(0, ROWS)], ld_sem.at[2 + lm]
        )
        c.start()
        t_copies.append(c)
    y_copy = pltpu.make_async_copy(tgt_hbm, tgt, ld_sem.at[1])
    y_copy.start()

    barrier = pltpu.get_barrier_semaphore()
    for o in range(1, G):
        pl.semaphore_signal(
            barrier, inc=1, device_id=dev("member", (me + o) % G), device_id_type=pl.DeviceIdType.MESH
        )
    for o in range(1, L):
        pl.semaphore_signal(
            barrier, inc=1, device_id=dev("lat", (lat + o) % L), device_id_type=pl.DeviceIdType.MESH
        )

    C = wfull.shape[1]
    lane = iota((1, LANES), 1)
    column = jnp.zeros((1, LANES), jnp.int32)
    for s in range(SEL):
        column = jnp.where(lane // PIX == s, chan_ref[s] * PIX + lane % PIX, column)
    pick = (iota((C, LANES), 0) == column).astype(F32).astype(BF16)
    if RP > ROWS:
        for lm in range(LM):
            tok[lm, pl.ds(ROWS, RP - ROWS), :] = jnp.zeros((RP - ROWS, D), BF16)
    w_copy.wait()
    head[...] = jnp.dot(wfull[...], pick, preferred_element_type=F32).astype(BF16)
    for c in t_copies:
        c.wait()
    pl.semaphore_wait(barrier, G - 1 + L - 1)

    def chunk(index):
        return pl.ds(pl.multiple_of(index * CH, 16), CH)

    def chip_rows(index):
        return pl.ds(pl.multiple_of(index * (2 * CH), 16), 2 * CH)

    def mem(device):
        return pl.ds(device * LM, LM)

    def predict(d):
        for lm in range(LM):
            fields[me * LM + lm, chunk(d), :] = jnp.dot(
                tok[lm, chunk(d), :], head[...], preferred_element_type=F32
            ).astype(BF16)

    p1 = []
    for o in [o for o in range(2, G)] + [1]:
        if o == 1:
            d = mate
        else:
            d = ((xc + o // 2) % X) * 2 + (core + o % 2) % 2
        predict(d)
        part = fields.at[mem(me), chunk(d)]
        c = remote(part, part, p1_s.at[o], p1_r.at[o], "member", d)
        c.start()
        p1.append(c)
    predict(me)

    def mate_own(o, owner):
        rows = chunk(owner) if o == 0 else chip_rows((xc + o) % X)
        part = fields.at[mem(owner), rows]
        return remote(part, part, i_s.at[o], i_r.at[o], "member", mate)

    i_c = [mate_own(o, me) for o in range(X)]

    lane8 = iota((8, LANES), 1)
    row8 = iota((8, LANES), 0)
    pixel = jnp.zeros((8, LANES), F32)
    for r in range(BANDS):
        pixel = jnp.where(row8 == r, band_ref[r].astype(F32) * P_SIZE, pixel)
    pixel = pixel + ((lane8 % PIX) // P_SIZE).astype(F32) + 0.5
    weights = jnp.cos((90.0 - 0.25 * pixel) * (math.pi / 180.0))
    root = jnp.sqrt(weights)
    for r in range(BANDS):
        wq[pl.ds(r * COLS, COLS), :] = jnp.broadcast_to(root[r : r + 1], (COLS, LANES))
    if RP > ROWS:
        wq[pl.ds(ROWS, RP - ROWS), :] = jnp.zeros((RP - ROWS, LANES), F32)
        yal[pl.ds(ROWS, RP - ROWS), :] = jnp.zeros((RP - ROWS, LANES), F32)
    weight_part = jnp.sum(jnp.where(row8 < BANDS, weights, 0.0), axis=0, keepdims=True) * (
        float(COLS) / float(G)
    )
    y_copy.wait()
    grid_rows = BANDS * P_SIZE
    KT = SEL * grid_rows
    values = tgt[...]
    high = values.astype(BF16)
    low = (values - high.astype(F32)).astype(BF16)
    k_id = iota((KT, LANES), 0)
    n_id = iota((KT, LANES), 1)
    for r in range(BANDS):
        place = (
            ((k_id // grid_rows) == (n_id // PIX))
            & ((k_id % grid_rows) == (r * P_SIZE + (n_id % PIX) // P_SIZE))
        ).astype(F32).astype(BF16)
        dims = (((0,), (0,)), ((), ()))
        wide[...] = lax.dot_general(high, place, dims, preferred_element_type=F32) + lax.dot_general(
            low, place, dims, preferred_element_type=F32
        )
        aligned = jnp.zeros((COLS, LANES), F32)
        phase = iota((COLS, LANES), 1) % P_SIZE
        for j in range(P_SIZE):
            aligned = jnp.where(phase == j, wide[pl.ds(j, COLS, stride=P_SIZE), :], aligned)
        yal[pl.ds(r * COLS, COLS), :] = aligned
    head_t[...] = head[...].astype(F32).T.astype(BF16)
    rsum[...] = jnp.zeros(rsum.shape, F32)
    rsum[pl.ds(NBP - 1 if NBP > M + 1 else 0, 1), :] = weight_part
    wslot = NBP - 1 if NBP > M + 1 else 0

    for c in p1:
        c.wait_recv()

    x_c = []
    for o in range(1, X):
        for o2 in range(X):
            if o2 != o:
                part = fields.at[mem(me), chip_rows((xc + o2) % X)]
                c = remote(part, part, x_s.at[o, o2], x_r.at[o, o2], "member", ((xc + o) % X) * 2 + core)
                c.start()
                x_c.append((o, o2, c))
    for c in i_c:
        c.start()
    ii_c = []
    for o in range(1, X):
        chip = (xc + o) % X
        part = fields.at[pl.ds(chip * (2 * LM), 2 * LM), chunk(me)]
        c = remote(part, part, ii_s.at[o], ii_r.at[o], "member", mate)
        c.start()
        ii_c.append(c)

    pairs = [(a, b) for a in range(M) for b in range(a + 1, M + 1)]
    for first in range(0, len(pairs), 36):
        group = pairs[first : first + 36]
        used = sorted({a for pair in group for a in pair})

        def gap_step(k, sums, group=group, used=used):
            start = pl.multiple_of(me * CH + k * 16, 16)
            root_rows = wq[pl.ds(start, 16), :]
            loaded = {}
            for b in used:
                if b < M:
                    loaded[b] = fields[b, pl.ds(start, 16), :].astype(F32) * root_rows
                else:
                    loaded[b] = yal[pl.ds(start, 16), :] * root_rows
            sums = list(sums)
            for half in range(2):
                part = {b: loaded[b][half * 8 : half * 8 + 8] for b in used}
                for n, (a, b) in enumerate(group):
                    delta = part[a] - part[b]
                    sums[n] = sums[n] + delta * delta
            return tuple(sums)

        zero = jnp.zeros((8, LANES), F32)
        sums = lax.fori_loop(0, CH // 16, gap_step, tuple(zero for _ in group))
        for n, (a, b) in enumerate(group):
            line = jnp.sum(sums[n], axis=0, keepdims=True)
            rsum[pl.ds(a * NBP + b, 1), :] = line
            if b < M:
                rsum[pl.ds(b * NBP + a, 1), :] = line

    channel = (iota((SEL, LANES), 0) == iota((SEL, LANES), 1) // PIX).astype(F32)
    abuf[lat] = lax.dot_general(
        channel, rsum[...], (((1,), (1,)), ((), ())), precision=HIGH, preferred_element_type=F32
    )
    a_c = []
    for o in range(1, L):
        c = remote(abuf.at[lat], abuf.at[lat], a_s.at[o], a_r.at[o], "lat", (lat + o) % L)
        c.start()
        a_c.append(c)

    iii_c = []
    for o, o2, c in x_c:
        c.wait_recv()
        chip = (xc + X - o) % X
        part = fields.at[mem(chip * 2 + core), chip_rows((chip + o2) % X)]
        q = remote(part, part, iii_s.at[o, o2], iii_r.at[o, o2], "member", mate)
        q.start()
        iii_c.append(q)

    for c in a_c:
        c.wait_recv()
    total = abuf[0]
    for l in range(1, L):
        total = total + abuf[l]
    bbuf[me] = total
    b_c = []
    for o in range(1, G):
        c = remote(bbuf.at[me], bbuf.at[me], b_s.at[o], b_r.at[o], "member", (me + o) % G)
        c.start()
        b_c.append(c)
    for c in b_c:
        c.wait_recv()
    total = bbuf[0]
    for g in range(1, G):
        total = total + bbuf[g]

    pair_lane = iota((SEL, NL), 1)
    a_id = pair_lane // NBP
    b_id = pair_lane % NBP
    weight_sum = jnp.sum(jnp.where(pair_lane == wslot, total, 0.0), axis=1, keepdims=True)
    gap = jnp.where((b_id <= M) & (a_id != b_id), total / weight_sum, 0.0)
    distance = jnp.sqrt(jnp.abs(gap) + EPSILON)
    sign = jnp.where(gap > 0.0, 1.0, jnp.where(gap < 0.0, -1.0, 0.0))
    inverse = sign / distance
    share = jnp.where(b_id < M, -1.0 / (2.0 * M * M), jnp.where(b_id == M, 1.0 / M, 0.0))
    energy_ref[...] = jnp.sum(
        jnp.sum(distance * share, axis=1, keepdims=True), axis=0, keepdims=True
    )
    crow[...] = lax.dot_general(
        inverse, channel, (((0,), (0,)), ((), ())), precision=HIGH, preferred_element_type=F32
    )
    scale = float(M * BANDS * L * P_SIZE * COLS * P_SIZE)
    one_weight = weight_sum[0:1, :]
    b_row = iota((NBP, LANES), 0)
    coefs = []
    for lm in range(LM):
        m = me * LM + lm
        inv = crow[pl.ds(pl.multiple_of(m * NBP, 8), NBP), :]
        pair_terms = jnp.where(b_row < M, inv, 0.0) * (1.0 / (M * M))
        own_terms = inv[M : M + 1] * (1.0 / M)
        add = own_terms - jnp.sum(pair_terms, axis=0, keepdims=True)
        coef = pair_terms + jnp.where(b_row == m, add, 0.0) - jnp.where(b_row == M, own_terms, 0.0)
        coefs.append(coef * (scale / one_weight))

    for o in range(X):
        mate_own(o, mate).wait_recv()
    for c in ii_c:
        c.wait_recv()
    for c in iii_c:
        c.wait_recv()

    lines = [[coefs[lm][b : b + 1] for b in range(M + 1)] for lm in range(LM)]

    def combine(k, carry):
        start = pl.multiple_of(k * 16, 16)
        root_rows = wq[pl.ds(start, 16), :]
        row_weight = root_rows * root_rows
        stacked = [fields[b, pl.ds(start, 16), :].astype(F32) for b in range(M)]
        stacked.append(yal[pl.ds(start, 16), :])
        for lm in range(LM):
            acc = stacked[0] * lines[lm][0]
            for b in range(1, M + 1):
                acc = acc + stacked[b] * lines[lm][b]
            up[lm, pl.ds(start, 16), :] = (acc * row_weight).astype(BF16)
        return carry

    lax.fori_loop(0, RP // 16, combine, 0)
    for lm in range(LM):
        up_t[lm] = up[lm].T

    def head_block(d):
        cols = pl.ds(pl.multiple_of(d * DB, 128), DB)
        acc = jnp.dot(up_t[0], tok[0, :, cols], preferred_element_type=F32)
        for lm in range(1, LM):
            acc = acc + jnp.dot(up_t[lm], tok[lm, :, cols], preferred_element_type=F32)
        return acc.T

    r1_c = []
    for o in [o for o in range(2, G)] + [1]:
        if o == 1:
            d = mate
        else:
            d = ((xc + o // 2) % X) * 2 + (core + o % 2) % 2
        s1[o] = head_block(d).astype(BF16)
        c = remote(s1.at[o], r1.at[o], r1_s.at[o], r1_r.at[o], "member", d)
        c.start()
        r1_c.append((o, c))
    total_block = head_block(me)

    parts = 3 if ROWS % 48 == 0 else 1
    step = ROWS // parts

    def back(lm, n):
        rows = pl.ds(n * step, step)
        gout[lm, rows, :] = jnp.dot(
            up[lm, rows, :], head_t[...], preferred_element_type=F32
        ).astype(BF16)
        c = pltpu.make_async_copy(
            gout.at[lm, rows], gtok_hbm.at[lm, rows], out_s.at[lm * parts + n]
        )
        c.start()
        return c

    jobs = [(lm, n) for lm in range(LM) for n in range(parts)]
    cut = len(jobs) // 2
    o_c = [back(*job) for job in jobs[:cut]]
    for o, c in r1_c:
        c.wait_recv()
    for o in range(1, G):
        total_block = total_block + r1[o].astype(F32)
    for l in range(L):
        piece = total_block[l * SB : (l + 1) * SB]
        own[l] = piece
        s2[l] = piece.astype(BF16)
    r2_c = []
    for o in range(1, L):
        l = (lat + o) % L
        c = remote(s2.at[l], r2.at[o], r2_s.at[o], r2_r.at[o], "lat", l)
        c.start()
        r2_c.append(c)
    o_c += [back(*job) for job in jobs[cut:]]
    for c in r2_c:
        c.wait_recv()
    result = own[lat]
    for o in range(1, L):
        result = result + r2[o].astype(F32)
    token_total = M * BANDS * L * COLS
    gw_ref[...] = result * (1.0 / math.sqrt(float(token_total)))

    for c in o_c:
        c.wait()
    for c in p1 + i_c + ii_c + iii_c + a_c + b_c + r2_c:
        c.wait_send()
    for _, _, c in x_c:
        c.wait_send()
    for _, c in r1_c:
        c.wait_send()


def shards(tokens, weight, channels, band_rows, target):
    LM, BANDS, COLS, D = tokens.shape
    G = lax.axis_size("member")
    L = lax.axis_size("lat")
    X = G // 2
    M = G * LM
    ROWS = BANDS * COLS
    RP = round_up(ROWS, 16 * G)
    NBP = round_up(M + 1, 8)
    NL = M * NBP
    DB = D // G
    SB = DB // L
    KT = SEL * BANDS * P_SIZE
    dma = pltpu.SemaphoreType.DMA
    parts = 3 if ROWS % 48 == 0 else 1
    any_spec = pl.BlockSpec(memory_space=pl.ANY)
    smem = pl.BlockSpec(memory_space=pltpu.SMEM)
    vmem = pl.BlockSpec(memory_space=pltpu.VMEM)
    energy, grad_tokens, grad_weight = pl.pallas_call(
        functools.partial(body, G, L, LM, BANDS, COLS),
        out_shape=(
            jax.ShapeDtypeStruct((1, 1), F32),
            jax.ShapeDtypeStruct((LM, ROWS, D), BF16),
            jax.ShapeDtypeStruct((SB, LANES), F32),
        ),
        in_specs=[smem, smem, any_spec, any_spec, any_spec],
        out_specs=(vmem, any_spec, vmem),
        scratch_shapes=[
            pltpu.VMEM((LM, RP, D), BF16),
            pltpu.VMEM(weight.shape, BF16),
            pltpu.VMEM((D, LANES), BF16),
            pltpu.VMEM((LANES, D), BF16),
            pltpu.VMEM((KT, COLS * P_SIZE), F32),
            pltpu.VMEM((COLS * P_SIZE, LANES), F32),
            pltpu.VMEM((RP, LANES), F32),
            pltpu.VMEM((RP, LANES), F32),
            pltpu.VMEM((M, RP, LANES), BF16),
            pltpu.VMEM((NL, LANES), F32),
            pltpu.VMEM((SEL, NL), F32),
            pltpu.VMEM((L, SEL, NL), F32),
            pltpu.VMEM((G, SEL, NL), F32),
            pltpu.VMEM((NL, LANES), F32),
            pltpu.VMEM((LM, RP, LANES), BF16),
            pltpu.VMEM((LM, LANES, RP), BF16),
            pltpu.VMEM((LM, ROWS, D), BF16),
            pltpu.VMEM((G, DB, LANES), BF16),
            pltpu.VMEM((G, DB, LANES), BF16),
            pltpu.VMEM((L, SB, LANES), F32),
            pltpu.VMEM((L, SB, LANES), BF16),
            pltpu.VMEM((L, SB, LANES), BF16),
            dma((2 + LM,)),
            dma((G,)),
            dma((G,)),
            dma((X, X)),
            dma((X, X)),
            dma((X,)),
            dma((X,)),
            dma((X,)),
            dma((X,)),
            dma((X, X)),
            dma((X, X)),
            dma((L,)),
            dma((L,)),
            dma((G,)),
            dma((G,)),
            dma((G,)),
            dma((G,)),
            dma((L,)),
            dma((L,)),
            dma((LM * parts,)),
        ],
        compiler_params=pltpu.CompilerParams(
            collective_id=0, has_side_effects=True, vmem_limit_bytes=VMEM_LIMIT
        ),
    )(
        channels,
        band_rows,
        tokens.reshape(LM, ROWS, D),
        weight,
        target.reshape(KT, COLS * P_SIZE),
    )
    return (energy.reshape(()), grad_tokens.reshape(tokens.shape), grad_weight)


def solution(mesh):
    placed = (P("member", "lat", None, None), P(), P(), P("lat"), P(None, "lat", None))
    return jax.shard_map(
        shards,
        mesh=mesh,
        in_specs=placed,
        out_specs=(P(), P("member", "lat", None, None), P(("member", "lat"), None)),
        check_vma=False,
    )
```

time: 249 us -> 47.3 us (0.19)
  waiting for transfers between devices: 134 us -> 0 us
  blocking collectives: 39 us -> 0 us
  Pallas kernels: 0 us -> 33.6 us
  matrix products: 27.3 us -> 0 us
  local copies, waits for them, and re-layouts: 25.3 us -> 11.1 us
  between operations: 16.6 us -> 2.4 us
  other arithmetic: 5.91 us -> 0 us
    unnamed x3 -> x0, waiting for transfers between devices: 125 us -> none
    psum x1 -> x0, blocking collectives: 39 us -> none  [shards(): lax.psum((partial_gram, jnp.sum(cell_weight) * 1.0), 'lat')]
    pallas_call x0 -> x1, Pallas kernels: none -> 33.6 us  [shards(): pl.pallas_call(functools.partial(body, G, L, LM, BANDS, COLS), out_shape=...]
    dot_general x5 -> x0, matrix products: 27.3 us -> none  [the longest x1 13 us: weighted_gram(): jnp.einsum('atsp,btsp->sab', stacked * slice_weight[None, :, None, :], st...]
    all_gather x1 -> x0, waiting for transfers between devices: 9.65 us -> none  [shards(): gathered = lax.all_gather(field, 'member', axis=0, tiled=True)]
    transpose x1 -> x0, local copies, waits for them, and re-layouts: 5.06 us -> none  [shards(): aligned = target.reshape(SEL, band_count, P_SIZE, column_count, P_SIZE).t...]
    gather x3 -> x0, local copies, waits for them, and re-layouts: 4.77 us -> none  [the longest x1 3.16 us: shards(): head_weight = jnp.take(weight, columns, axis=1)]
    reshape x1 -> x0, local copies, waits for them, and re-layouts: 3.19 us -> none  [stack_fields(): member_fields.astype(jnp.float32)]
  transfers between devices with their start and end apart: 2 -> 0, of which waited for: 2 -> 0; matrix products, arithmetic and copies ran while one was open for 7% -> 0% of each run, Pallas kernels for 0% -> 0%
where the time goes in v1:
time: 47.3 us; the launch traced here: 47 us
  Pallas kernels  33.6 us (71%)
  local copies, waits for them, and re-layouts  11.1 us (23%)
  between operations  2.4 us (5%)
    pallas_call x1, Pallas kernels, shards(): pl.pallas_call(functools.partial(body, G, L, LM, BANDS, COLS), out_shape=...  33.6 us
    unnamed x13, local copies, waits for them, and re-layouts  11.1 us

profile of v1, /device:TPU:0, one launch (start us, length us, event | category | flops | bytes accessed | tf_op | source)
XLA Modules:
  0.0 47.0 jit_solution(11952672955986656306)
XLA Ops:
  0.6 0.0 copy-start.2
  0.6 0.0 copy-start.4
  0.7 0.0 copy-start.3
  0.7 3.3 %copy.8.w_hbm = bf16[1024,1328]{1,0:T(8,128)(2,1)S(1)} copy(bf16[1024,1328]{0,1:T(8,128)(2,1)} %param.6) | data formatting | bytes 5439488 | tf_op args[1]
  4.0 0.0 copy-done.2
  4.0 0.0 copy-done.4
  4.0 0.0 copy-done.3
  4.0 0.0 copy-start
  4.0 1.8 %copy-done = bf16[2,2,360,1024]{3,2,1,0:T(8,128)(2,1)S(1)} copy-done((bf16[2,2,360,1024]{3,2,1,0:T(8,128)(2,1)S(1)}, bf16[2,2,360,1024]{3,2,1,0:T(8,128)(2,1)}, u32[]{:S(2)}) %copy-start) | copy-done | bytes 2949144
  5.9 33.6 %shard_map.76 = (f32[1,1]{1,0:T(1,128)}, bf16[2,720,1024]{2,1,0:T(8,128)(2,1)S(1)}, f32[32,128]{1,0:T(8,128)S(1)}) custom-call(s32[8]{0:T(128)S(1)} %copy-done.3, s32[2]{0:T(128)S(1)} %copy-done.4, bf16[2,720,1024]{2,1,0:T(8,128)(2,1)S(1)} %bitcast.4, bf16[1024,1328]{1,0:T(8,128)(2,1)S(1)} %copy.8.w_hbm, f32[64,1440]{1,0:T(8,128)S(1)} %bitcast.6), custom_call_target="tpu_custom_call" | custom-call | tf_op jit(solution)/shard_map/pallas_call | solution.py:459
  39.4 0.0 copy-start.1
  39.4 1.6 %copy-done.1 = bf16[2,720,1024]{2,1,0:T(8,128)(2,1)} copy-done((bf16[2,720,1024]{2,1,0:T(8,128)(2,1)}, bf16[2,720,1024]{2,1,0:T(8,128)(2,1)S(1)}, u32[]{:S(2)}) %copy-start.1) | copy-done | bytes 2949144
  41.6 3.7 %copy.13 = bf16[2,2,360,1024]{3,2,1,0:T(8,128)(2,1)} copy(bf16[2,2,360,1024]{3,2,1,0:T(8,128)(2,1)} %bitcast.5) | data formatting | bytes 5898240
  45.3 0.6 %copy.14 = f32[32,128]{1,0:T(8,128)} copy(f32[32,128]{1,0:T(8,128)S(1)} %get-tuple-element.14) | data formatting | bytes 32768
Async XLA Ops:
  0.6 3.4 %copy-start.2 = (f32[8,8,1440]{2,1,0:T(8,128)S(1)}, f32[8,8,1440]{2,1,0:T(8,128)}, u32[]{:S(2)}) copy-start(f32[8,8,1440]{2,1,0:T(8,128)} %param.9) | copy-start | bytes 1105924
  0.6 3.4 %copy-start.4 = (s32[2]{0:T(128)S(1)}, s32[2]{0:T(128)}, u32[]{:S(2)}) copy-start(s32[2]{0:T(128)} %band_ref.1) | copy-start | bytes 28
  0.7 3.4 %copy-start.3 = (s32[8]{0:T(128)S(1)}, s32[8]{0:T(128)}, u32[]{:S(2)}) copy-start(s32[8]{0:T(128)} %chan_ref.1) | copy-start | bytes 100
  4.0 1.8 %copy-start = (bf16[2,2,360,1024]{3,2,1,0:T(8,128)(2,1)S(1)}, bf16[2,2,360,1024]{3,2,1,0:T(8,128)(2,1)}, u32[]{:S(2)}) copy-start(bf16[2,2,360,1024]{3,2,1,0:T(8,128)(2,1)} %param.5) | copy-start | bytes 8847364
  39.4 1.6 %copy-start.1 = (bf16[2,720,1024]{2,1,0:T(8,128)(2,1)}, bf16[2,720,1024]{2,1,0:T(8,128)(2,1)S(1)}, u32[]{:S(2)}) copy-start(bf16[2,720,1024]{2,1,0:T(8,128)(2,1)S(1)} %get-tuple-element.7) | copy-start | bytes 8847364

commit v2 on v1

--- a/solution.py
+++ b/solution.py
@@ -16,7 +16,7 @@
 F32 = jnp.float32
 BF16 = jnp.bfloat16
 HIGH = lax.Precision.HIGHEST
-VMEM_LIMIT = 40 * 1024 * 1024
+VMEM_LIMIT = 121 * 512 * 1024
 
 
 def round_up(value, step):
@@ -33,31 +33,30 @@
     LM,
     BANDS,
     COLS,
-    chan_ref,
-    band_ref,
+    chan_hbm,
+    band_hbm,
     tok_hbm,
     w_hbm,
     tgt_hbm,
     energy_ref,
-    gtok_hbm,
+    gout,
     gw_ref,
+    chan_ref,
+    band_ref,
     tok,
     wfull,
-    head,
-    head_t,
     tgt,
     wide,
     yal,
     wq,
     fields,
     rsum,
-    msg,
     abuf,
     bbuf,
     crow,
     up,
+    head_t,
     up_t,
-    gout,
     s1,
     r1,
     own,
@@ -82,7 +81,6 @@
     r1_r,
     r2_s,
     r2_r,
-    out_s,
 ):
     X = G // 2
     M = G * LM
@@ -115,13 +113,19 @@
 
     w_copy = pltpu.make_async_copy(w_hbm, wfull, ld_sem.at[0])
     w_copy.start()
+    c_copy = pltpu.make_async_copy(chan_hbm, chan_ref, ld_sem.at[2 + LM * G])
+    c_copy.start()
+    r_copy = pltpu.make_async_copy(band_hbm, band_ref, ld_sem.at[3 + LM * G])
+    r_copy.start()
     t_copies = []
-    for lm in range(LM):
-        c = pltpu.make_async_copy(
-            tok_hbm.at[lm], tok.at[lm, pl.ds(0, ROWS)], ld_sem.at[2 + lm]
-        )
-        c.start()
-        t_copies.append(c)
+    for g in range(G):
+        for lm in range(LM):
+            rows = pl.ds(g * CH, min(CH, ROWS - g * CH))
+            c = pltpu.make_async_copy(
+                tok_hbm.at[lm, rows], tok.at[lm, rows], ld_sem.at[2 + g * LM + lm]
+            )
+            c.start()
+            t_copies.append(c)
     y_copy = pltpu.make_async_copy(tgt_hbm, tgt, ld_sem.at[1])
     y_copy.start()
 
@@ -135,17 +139,14 @@
             barrier, inc=1, device_id=dev("lat", (lat + o) % L), device_id_type=pl.DeviceIdType.MESH
         )
 
-    C = wfull.shape[1]
-    lane = iota((1, LANES), 1)
-    column = jnp.zeros((1, LANES), jnp.int32)
-    for s in range(SEL):
-        column = jnp.where(lane // PIX == s, chan_ref[s] * PIX + lane % PIX, column)
-    pick = (iota((C, LANES), 0) == column).astype(F32).astype(BF16)
     if RP > ROWS:
         for lm in range(LM):
             tok[lm, pl.ds(ROWS, RP - ROWS), :] = jnp.zeros((RP - ROWS, D), BF16)
+    c_copy.wait()
+    r_copy.wait()
     w_copy.wait()
-    head[...] = jnp.dot(wfull[...], pick, preferred_element_type=F32).astype(BF16)
+    for s in range(SEL):
+        head_t[pl.ds(s * PIX, PIX), :] = wfull[chan_ref[s]]
     for c in t_copies:
         c.wait()
     pl.semaphore_wait(barrier, G - 1 + L - 1)
@@ -161,8 +162,11 @@
 
     def predict(d):
         for lm in range(LM):
-            fields[me * LM + lm, chunk(d), :] = jnp.dot(
-                tok[lm, chunk(d), :], head[...], preferred_element_type=F32
+            fields[me * LM + lm, chunk(d), :] = lax.dot_general(
+                tok[lm, chunk(d), :],
+                head_t[...],
+                (((1,), (1,)), ((), ())),
+                preferred_element_type=F32,
             ).astype(BF16)
 
     p1 = []
@@ -223,13 +227,12 @@
         for j in range(P_SIZE):
             aligned = jnp.where(phase == j, wide[pl.ds(j, COLS, stride=P_SIZE), :], aligned)
         yal[pl.ds(r * COLS, COLS), :] = aligned
-    head_t[...] = head[...].astype(F32).T.astype(BF16)
     rsum[...] = jnp.zeros(rsum.shape, F32)
     rsum[pl.ds(NBP - 1 if NBP > M + 1 else 0, 1), :] = weight_part
     wslot = NBP - 1 if NBP > M + 1 else 0
 
-    for c in p1:
-        c.wait_recv()
+    for c in p1[:-1]:
+        c.wait_send()
 
     x_c = []
     for o in range(1, X):
@@ -239,16 +242,8 @@
                 c = remote(part, part, x_s.at[o, o2], x_r.at[o, o2], "member", ((xc + o) % X) * 2 + core)
                 c.start()
                 x_c.append((o, o2, c))
-    for c in i_c:
-        c.start()
-    ii_c = []
-    for o in range(1, X):
-        chip = (xc + o) % X
-        part = fields.at[pl.ds(chip * (2 * LM), 2 * LM), chunk(me)]
-        c = remote(part, part, ii_s.at[o], ii_r.at[o], "member", mate)
-        c.start()
-        ii_c.append(c)
-
+    for c in p1:
+        c.wait_recv()
     pairs = [(a, b) for a in range(M) for b in range(a + 1, M + 1)]
     for first in range(0, len(pairs), 36):
         group = pairs[first : first + 36]
@@ -289,14 +284,15 @@
         c.start()
         a_c.append(c)
 
-    iii_c = []
-    for o, o2, c in x_c:
-        c.wait_recv()
-        chip = (xc + X - o) % X
-        part = fields.at[mem(chip * 2 + core), chip_rows((chip + o2) % X)]
-        q = remote(part, part, iii_s.at[o, o2], iii_r.at[o, o2], "member", mate)
-        q.start()
-        iii_c.append(q)
+    for c in i_c:
+        c.start()
+    ii_c = []
+    for o in range(1, X):
+        chip = (xc + o) % X
+        part = fields.at[pl.ds(chip * (2 * LM), 2 * LM), chunk(me)]
+        c = remote(part, part, ii_s.at[o], ii_r.at[o], "member", mate)
+        c.start()
+        ii_c.append(c)
 
     for c in a_c:
         c.wait_recv()
@@ -309,6 +305,15 @@
         c = remote(bbuf.at[me], bbuf.at[me], b_s.at[o], b_r.at[o], "member", (me + o) % G)
         c.start()
         b_c.append(c)
+    iii_c = []
+    for o, o2, c in x_c:
+        c.wait_recv()
+        chip = (xc + X - o) % X
+        part = fields.at[mem(chip * 2 + core), chip_rows((chip + o2) % X)]
+        q = remote(part, part, iii_s.at[o, o2], iii_r.at[o, o2], "member", mate)
+        q.start()
+        iii_c.append(q)
+
     for c in b_c:
         c.wait_recv()
     total = bbuf[0]
@@ -376,19 +381,27 @@
             acc = acc + jnp.dot(up_t[lm], tok[lm, :, cols], preferred_element_type=F32)
         return acc.T
 
+    theirs = []
+    for o in list(range(1, X)) + [0]:
+        s1[o] = head_block(((xc + o) % X) * 2 + 1 - core).astype(BF16)
+        c = remote(s1.at[o], r1.at[o], r1_s.at[o], r1_r.at[o], "member", mate)
+        c.start()
+        theirs.append(c)
     r1_c = []
-    for o in [o for o in range(2, G)] + [1]:
-        if o == 1:
-            d = mate
-        else:
-            d = ((xc + o // 2) % X) * 2 + (core + o % 2) % 2
-        s1[o] = head_block(d).astype(BF16)
-        c = remote(s1.at[o], r1.at[o], r1_s.at[o], r1_r.at[o], "member", d)
+    for o in range(1, X):
+        block = head_block(((xc + o) % X) * 2 + core)
+        theirs[o - 1].wait_recv()
+        s1[X + o] = (block + r1[o].astype(F32)).astype(BF16)
+        c = remote(
+            s1.at[X + o], r1.at[X + o], r1_s.at[X + o], r1_r.at[X + o], "member", ((xc + o) % X) * 2 + core
+        )
         c.start()
         r1_c.append((o, c))
     total_block = head_block(me)
-
-    parts = 3 if ROWS % 48 == 0 else 1
+    theirs[X - 1].wait_recv()
+    total_block = total_block + r1[0].astype(F32)
+
+    parts = 6 if ROWS % 96 == 0 else (3 if ROWS % 48 == 0 else 1)
     step = ROWS // parts
 
     def back(lm, n):
@@ -396,19 +409,15 @@
         gout[lm, rows, :] = jnp.dot(
             up[lm, rows, :], head_t[...], preferred_element_type=F32
         ).astype(BF16)
-        c = pltpu.make_async_copy(
-            gout.at[lm, rows], gtok_hbm.at[lm, rows], out_s.at[lm * parts + n]
-        )
-        c.start()
-        return c
 
     jobs = [(lm, n) for lm in range(LM) for n in range(parts)]
     cut = len(jobs) // 2
-    o_c = [back(*job) for job in jobs[:cut]]
+    for job in jobs[:cut]:
+        back(*job)
     for o, c in r1_c:
         c.wait_recv()
-    for o in range(1, G):
-        total_block = total_block + r1[o].astype(F32)
+    for o in range(1, X):
+        total_block = total_block + r1[X + o].astype(F32)
     for l in range(L):
         piece = total_block[l * SB : (l + 1) * SB]
         own[l] = piece
@@ -419,7 +428,8 @@
         c = remote(s2.at[l], r2.at[o], r2_s.at[o], r2_r.at[o], "lat", l)
         c.start()
         r2_c.append(c)
-    o_c += [back(*job) for job in jobs[cut:]]
+    for job in jobs[cut:]:
+        back(*job)
     for c in r2_c:
         c.wait_recv()
     result = own[lat]
@@ -428,14 +438,33 @@
     token_total = M * BANDS * L * COLS
     gw_ref[...] = result * (1.0 / math.sqrt(float(token_total)))
 
-    for c in o_c:
-        c.wait()
-    for c in p1 + i_c + ii_c + iii_c + a_c + b_c + r2_c:
+    p1[-1].wait_send()
+    for c in i_c + ii_c + iii_c + a_c + b_c + theirs + r2_c:
         c.wait_send()
     for _, _, c in x_c:
         c.wait_send()
     for _, c in r1_c:
         c.wait_send()
+
+
+def finish(parts, energy_in, gout, gw_in, energy_hbm, gtok_hbm, gw_hbm, sems):
+    LM, ROWS, _ = gout.shape
+    step = ROWS // parts
+    copies = []
+    for lm in range(LM):
+        for n in range(parts):
+            rows = pl.ds(n * step, step)
+            c = pltpu.make_async_copy(
+                gout.at[lm, rows], gtok_hbm.at[lm, rows], sems.at[lm * parts + n]
+            )
+            c.start()
+            copies.append(c)
+    for n, (src, dst) in enumerate([(energy_in, energy_hbm), (gw_in, gw_hbm)]):
+        c = pltpu.make_async_copy(src, dst, sems.at[LM * parts + n])
+        c.start()
+        copies.append(c)
+    for c in copies:
+        c.wait()
 
 
 def shards(tokens, weight, channels, band_rows, target):
@@ -453,42 +482,40 @@
     KT = SEL * BANDS * P_SIZE
     dma = pltpu.SemaphoreType.DMA
     parts = 3 if ROWS % 48 == 0 else 1
-    any_spec = pl.BlockSpec(memory_space=pl.ANY)
-    smem = pl.BlockSpec(memory_space=pltpu.SMEM)
+    hbm = pl.BlockSpec(memory_space=pltpu.HBM)
     vmem = pl.BlockSpec(memory_space=pltpu.VMEM)
-    energy, grad_tokens, grad_weight = pl.pallas_call(
+    energy, gout, grad_weight = pl.pallas_call(
         functools.partial(body, G, L, LM, BANDS, COLS),
         out_shape=(
-            jax.ShapeDtypeStruct((1, 1), F32),
-            jax.ShapeDtypeStruct((LM, ROWS, D), BF16),
-            jax.ShapeDtypeStruct((SB, LANES), F32),
+            pltpu.VMEM((1, 1), F32),
+            pltpu.VMEM((LM, ROWS, D), BF16),
+            pltpu.VMEM((SB, LANES), F32),
         ),
-        in_specs=[smem, smem, any_spec, any_spec, any_spec],
-        out_specs=(vmem, any_spec, vmem),
+        in_specs=[hbm, hbm, hbm, hbm, hbm],
+        out_specs=(vmem, vmem, vmem),
         scratch_shapes=[
+            pltpu.SMEM(channels.shape, jnp.int32),
+            pltpu.SMEM(band_rows.shape, jnp.int32),
             pltpu.VMEM((LM, RP, D), BF16),
-            pltpu.VMEM(weight.shape, BF16),
-            pltpu.VMEM((D, LANES), BF16),
-            pltpu.VMEM((LANES, D), BF16),
+            pltpu.VMEM((weight.shape[1] // PIX, PIX, D), BF16),
             pltpu.VMEM((KT, COLS * P_SIZE), F32),
             pltpu.VMEM((COLS * P_SIZE, LANES), F32),
             pltpu.VMEM((RP, LANES), F32),
             pltpu.VMEM((RP, LANES), F32),
             pltpu.VMEM((M, RP, LANES), BF16),
             pltpu.VMEM((NL, LANES), F32),
-            pltpu.VMEM((SEL, NL), F32),
             pltpu.VMEM((L, SEL, NL), F32),
             pltpu.VMEM((G, SEL, NL), F32),
             pltpu.VMEM((NL, LANES), F32),
             pltpu.VMEM((LM, RP, LANES), BF16),
+            pltpu.VMEM((LANES, D), BF16),
             pltpu.VMEM((LM, LANES, RP), BF16),
-            pltpu.VMEM((LM, ROWS, D), BF16),
             pltpu.VMEM((G, DB, LANES), BF16),
             pltpu.VMEM((G, DB, LANES), BF16),
             pltpu.VMEM((L, SB, LANES), F32),
             pltpu.VMEM((L, SB, LANES), BF16),
             pltpu.VMEM((L, SB, LANES), BF16),
-            dma((2 + LM,)),
+            dma((4 + LM * G,)),
             dma((G,)),
             dma((G,)),
             dma((X, X)),
@@ -507,7 +534,6 @@
             dma((G,)),
             dma((L,)),
             dma((L,)),
-            dma((LM * parts,)),
         ],
         compiler_params=pltpu.CompilerParams(
             collective_id=0, has_side_effects=True, vmem_limit_bytes=VMEM_LIMIT
@@ -516,9 +542,21 @@
         channels,
         band_rows,
         tokens.reshape(LM, ROWS, D),
-        weight,
+        weight.T.reshape(weight.shape[1] // PIX, PIX, D),
         target.reshape(KT, COLS * P_SIZE),
     )
+    energy, grad_tokens, grad_weight = pl.pallas_call(
+        functools.partial(finish, parts),
+        out_shape=(
+            jax.ShapeDtypeStruct((1, 1), F32),
+            jax.ShapeDtypeStruct((LM, ROWS, D), BF16),
+            jax.ShapeDtypeStruct((SB, LANES), F32),
+        ),
+        in_specs=[vmem] * 3,
+        out_specs=(hbm, hbm, hbm),
+        scratch_shapes=[dma((LM * parts + 2,))],
+        compiler_params=pltpu.CompilerParams(vmem_limit_bytes=4 * 1024 * 1024),
+    )(energy, gout, grad_weight)
     return (energy.reshape(()), grad_tokens.reshape(tokens.shape), grad_weight)
 
 

time: 47.3 us -> 34.1 us (0.72)
  local copies, waits for them, and re-layouts: 11.1 us -> 0 us
  between operations: 2.4 us -> 0.64 us
    unnamed x13 -> x0, local copies, waits for them, and re-layouts: 11.1 us -> none
    pallas_call x1, Pallas kernels: 33.6 us -> 31 us  [shards(): pl.pallas_call(functools.partial(body, G, L, LM, BANDS, COLS), out_shape=...]
    pallas_call x0 -> x1, Pallas kernels: none -> 2.29 us  [shards(): pl.pallas_call(functools.partial(finish, parts), out_shape=(jax.ShapeDtyp...]
where the time goes in v2:
time: 34.1 us; the launch traced here: 34 us
  Pallas kernels  33.3 us (98%)
  between operations  0.64 us (2%)
    pallas_call x1, Pallas kernels, shards(): pl.pallas_call(functools.partial(body, G, L, LM, BANDS, COLS), out_shape=...  31 us
    pallas_call x1, Pallas kernels, shards(): pl.pallas_call(functools.partial(finish, parts), out_shape=(jax.ShapeDtyp...  2.29 us

profile of v2, /device:TPU:0, one launch (start us, length us, event | category | flops | bytes accessed | tf_op | source)
XLA Modules:
  0.0 34.0 jit_solution(8910168315867692962)
XLA Ops:
  0.6 31.0 %shard_map.76 = (f32[1,1]{1,0:T(1,128)}, bf16[2,720,1024]{2,1,0:T(8,128)(2,1)S(1)}, f32[32,128]{1,0:T(8,128)S(1)}) custom-call(s32[8]{0:T(128)} %chan_hbm.1, s32[2]{0:T(128)} %band_hbm.1, bf16[2,720,1024]{2,1,0:T(8,128)(2,1)} %bitcast.7, bf16[83,16,1024]{2,1,0:T(8,128)(2,1)} %bitcast.8, f32[64,1440]{1,0:T(8,128)} %bitcast.9), custom_call_target="tpu_custom_call" | custom-call | tf_op jit(solution)/shard_map/pallas_call | solution.py:487
  31.7 2.3 %shard_map.77 = (f32[1,1]{1,0:T(1,128)}, bf16[2,720,1024]{2,1,0:T(8,128)(2,1)}, f32[32,128]{1,0:T(8,128)}) custom-call(f32[1,1]{1,0:T(1,128)} %get-tuple-element.9.energy_in, bf16[2,720,1024]{2,1,0:T(8,128)(2,1)S(1)} %get-tuple-element.10.gout, f32[32,128]{1,0:T(8,128)S(1)} %get-tuple-element.11.gw_in), custom_call_target="tpu_custom_call" | custom-call | tf_op jit(solution)/shard_map/pallas_call | solution.py:548

commit v3 on v2

--- a/solution.py
+++ b/solution.py
@@ -135,9 +135,13 @@
             barrier, inc=1, device_id=dev("member", (me + o) % G), device_id_type=pl.DeviceIdType.MESH
         )
     for o in range(1, L):
-        pl.semaphore_signal(
-            barrier, inc=1, device_id=dev("lat", (lat + o) % L), device_id_type=pl.DeviceIdType.MESH
-        )
+        for ox in range(X):
+            pl.semaphore_signal(
+                barrier,
+                inc=1,
+                device_id={"member": ((xc + ox) % X) * 2 + core, "lat": (lat + o) % L},
+                device_id_type=pl.DeviceIdType.MESH,
+            )
 
     if RP > ROWS:
         for lm in range(LM):
@@ -149,7 +153,7 @@
         head_t[pl.ds(s * PIX, PIX), :] = wfull[chan_ref[s]]
     for c in t_copies:
         c.wait()
-    pl.semaphore_wait(barrier, G - 1 + L - 1)
+    pl.semaphore_wait(barrier, G - 1 + (L - 1) * X)
 
     def chunk(index):
         return pl.ds(pl.multiple_of(index * CH, 16), CH)
@@ -387,19 +391,39 @@
         c = remote(s1.at[o], r1.at[o], r1_s.at[o], r1_r.at[o], "member", mate)
         c.start()
         theirs.append(c)
-    r1_c = []
-    for o in range(1, X):
-        block = head_block(((xc + o) % X) * 2 + core)
-        theirs[o - 1].wait_recv()
-        s1[X + o] = (block + r1[o].astype(F32)).astype(BF16)
-        c = remote(
-            s1.at[X + o], r1.at[X + o], r1_s.at[X + o], r1_r.at[X + o], "member", ((xc + o) % X) * 2 + core
-        )
-        c.start()
-        r1_c.append((o, c))
+    r2_c = []
+
+    def pieces(value, n):
+        for l in range(L):
+            s2[n, l] = value[l * SB : (l + 1) * SB].astype(BF16)
+
+    def deliver(ox):
+        for o in FAR if ox else [o for o in FAR if o]:
+            l = (lat + o) % L
+            c = pltpu.make_async_remote_copy(
+                src_ref=s2.at[ox, l],
+                dst_ref=r2.at[ox, o],
+                send_sem=r2_s.at[ox, o],
+                recv_sem=r2_r.at[ox, o],
+                device_id={"member": ((xc + ox) % X) * 2 + core, "lat": l},
+                device_id_type=pl.DeviceIdType.MESH,
+            )
+            c.start()
+            r2_c.append((ox, o, c))
+
+    FAR = sorted(range(L), key=lambda o: -min(o, L - o))
+    for ox in range(1, X):
+        block = head_block(((xc + ox) % X) * 2 + core)
+        theirs[ox - 1].wait_recv()
+        pieces(block + r1[ox].astype(F32), ox)
+        deliver(ox)
     total_block = head_block(me)
     theirs[X - 1].wait_recv()
     total_block = total_block + r1[0].astype(F32)
+    pieces(total_block, 0)
+    deliver(0)
+    for l in range(L):
+        own[l] = total_block[l * SB : (l + 1) * SB]
 
     parts = 6 if ROWS % 96 == 0 else (3 if ROWS % 48 == 0 else 1)
     step = ROWS // parts
@@ -414,36 +438,19 @@
     cut = len(jobs) // 2
     for job in jobs[:cut]:
         back(*job)
-    for o, c in r1_c:
-        c.wait_recv()
-    for o in range(1, X):
-        total_block = total_block + r1[X + o].astype(F32)
-    for l in range(L):
-        piece = total_block[l * SB : (l + 1) * SB]
-        own[l] = piece
-        s2[l] = piece.astype(BF16)
-    r2_c = []
-    for o in range(1, L):
-        l = (lat + o) % L
-        c = remote(s2.at[l], r2.at[o], r2_s.at[o], r2_r.at[o], "lat", l)
-        c.start()
-        r2_c.append(c)
     for job in jobs[cut:]:
         back(*job)
-    for c in r2_c:
-        c.wait_recv()
     result = own[lat]
-    for o in range(1, L):
-        result = result + r2[o].astype(F32)
+    for ox, o, c in r2_c:
+        c.wait_recv()
+        result = result + r2[ox, o].astype(F32)
     token_total = M * BANDS * L * COLS
     gw_ref[...] = result * (1.0 / math.sqrt(float(token_total)))
 
     p1[-1].wait_send()
-    for c in i_c + ii_c + iii_c + a_c + b_c + theirs + r2_c:
+    for c in i_c + ii_c + iii_c + a_c + b_c + theirs + [c for _, _, c in r2_c]:
         c.wait_send()
     for _, _, c in x_c:
-        c.wait_send()
-    for _, c in r1_c:
         c.wait_send()
 
 
@@ -510,11 +517,11 @@
             pltpu.VMEM((LM, RP, LANES), BF16),
             pltpu.VMEM((LANES, D), BF16),
             pltpu.VMEM((LM, LANES, RP), BF16),
-            pltpu.VMEM((G, DB, LANES), BF16),
-            pltpu.VMEM((G, DB, LANES), BF16),
+            pltpu.VMEM((X, DB, LANES), BF16),
+            pltpu.VMEM((X, DB, LANES), BF16),
             pltpu.VMEM((L, SB, LANES), F32),
-            pltpu.VMEM((L, SB, LANES), BF16),
-            pltpu.VMEM((L, SB, LANES), BF16),
+            pltpu.VMEM((X, L, SB, LANES), BF16),
+            pltpu.VMEM((X, L, SB, LANES), BF16),
             dma((4 + LM * G,)),
             dma((G,)),
             dma((G,)),
@@ -530,10 +537,10 @@
             dma((L,)),
             dma((G,)),
             dma((G,)),
-            dma((G,)),
-            dma((G,)),
-            dma((L,)),
-            dma((L,)),
+            dma((X,)),
+            dma((X,)),
+            dma((X, L)),
+            dma((X, L)),
         ],
         compiler_params=pltpu.CompilerParams(
             collective_id=0, has_side_effects=True, vmem_limit_bytes=VMEM_LIMIT

time: 34.1 us -> 32.8 us (0.962)
  Pallas kernels: 33.3 us -> 32 us
    pallas_call x1, Pallas kernels: 31 us -> 29.7 us  [shards(): pl.pallas_call(functools.partial(body, G, L, LM, BANDS, COLS), out_shape=...]
where the time goes in v3:
time: 32.8 us; the launch traced here: 32.6 us
  Pallas kernels  32 us (98%)
  between operations  0.64 us (2%)
    pallas_call x1, Pallas kernels, shards(): pl.pallas_call(functools.partial(body, G, L, LM, BANDS, COLS), out_shape=...  29.7 us
    pallas_call x1, Pallas kernels, shards(): pl.pallas_call(functools.partial(finish, parts), out_shape=(jax.ShapeDtyp...  2.29 us

profile of v3, /device:TPU:0, one launch (start us, length us, event | category | flops | bytes accessed | tf_op | source)
XLA Modules:
  0.0 32.6 jit_solution(7037609134084377108)
XLA Ops:
  0.6 29.7 %shard_map.76 = (f32[1,1]{1,0:T(1,128)}, bf16[2,720,1024]{2,1,0:T(8,128)(2,1)S(1)}, f32[32,128]{1,0:T(8,128)S(1)}) custom-call(s32[8]{0:T(128)} %chan_hbm.1, s32[2]{0:T(128)} %band_hbm.1, bf16[2,720,1024]{2,1,0:T(8,128)(2,1)} %bitcast.7, bf16[83,16,1024]{2,1,0:T(8,128)(2,1)} %bitcast.8, f32[64,1440]{1,0:T(8,128)} %bitcast.9), custom_call_target="tpu_custom_call" | custom-call | tf_op jit(solution)/shard_map/pallas_call | solution.py:494
  30.3 2.3 %shard_map.77 = (f32[1,1]{1,0:T(1,128)}, bf16[2,720,1024]{2,1,0:T(8,128)(2,1)}, f32[32,128]{1,0:T(8,128)}) custom-call(f32[1,1]{1,0:T(1,128)} %get-tuple-element.9.energy_in, bf16[2,720,1024]{2,1,0:T(8,128)(2,1)S(1)} %get-tuple-element.10.gout, f32[32,128]{1,0:T(8,128)S(1)} %get-tuple-element.11.gw_in), custom_call_target="tpu_custom_call" | custom-call | tf_op jit(solution)/shard_map/pallas_call | solution.py:555

commit v4 on v3

--- a/solution.py
+++ b/solution.py
@@ -111,6 +111,20 @@
             device_id_type=pl.DeviceIdType.MESH,
         )
 
+    barrier = pltpu.get_barrier_semaphore()
+    for o in range(1, G):
+        pl.semaphore_signal(
+            barrier, inc=1, device_id=dev("member", (me + o) % G), device_id_type=pl.DeviceIdType.MESH
+        )
+    for o in range(1, L):
+        for ox in range(X):
+            pl.semaphore_signal(
+                barrier,
+                inc=1,
+                device_id={"member": ((xc + ox) % X) * 2 + core, "lat": (lat + o) % L},
+                device_id_type=pl.DeviceIdType.MESH,
+            )
+
     w_copy = pltpu.make_async_copy(w_hbm, wfull, ld_sem.at[0])
     w_copy.start()
     c_copy = pltpu.make_async_copy(chan_hbm, chan_ref, ld_sem.at[2 + LM * G])
@@ -128,20 +142,6 @@
             t_copies.append(c)
     y_copy = pltpu.make_async_copy(tgt_hbm, tgt, ld_sem.at[1])
     y_copy.start()
-
-    barrier = pltpu.get_barrier_semaphore()
-    for o in range(1, G):
-        pl.semaphore_signal(
-            barrier, inc=1, device_id=dev("member", (me + o) % G), device_id_type=pl.DeviceIdType.MESH
-        )
-    for o in range(1, L):
-        for ox in range(X):
-            pl.semaphore_signal(
-                barrier,
-                inc=1,
-                device_id={"member": ((xc + ox) % X) * 2 + core, "lat": (lat + o) % L},
-                device_id_type=pl.DeviceIdType.MESH,
-            )
 
     if RP > ROWS:
         for lm in range(LM):
@@ -237,6 +237,8 @@
 
     for c in p1[:-1]:
         c.wait_send()
+    for c in p1:
+        c.wait_recv()
 
     x_c = []
     for o in range(1, X):
@@ -246,8 +248,6 @@
                 c = remote(part, part, x_s.at[o, o2], x_r.at[o, o2], "member", ((xc + o) % X) * 2 + core)
                 c.start()
                 x_c.append((o, o2, c))
-    for c in p1:
-        c.wait_recv()
     pairs = [(a, b) for a in range(M) for b in range(a + 1, M + 1)]
     for first in range(0, len(pairs), 36):
         group = pairs[first : first + 36]
@@ -283,7 +283,7 @@
         channel, rsum[...], (((1,), (1,)), ((), ())), precision=HIGH, preferred_element_type=F32
     )
     a_c = []
-    for o in range(1, L):
+    for o in sorted(range(1, L), key=lambda o: -min(o, L - o)):
         c = remote(abuf.at[lat], abuf.at[lat], a_s.at[o], a_r.at[o], "lat", (lat + o) % L)
         c.start()
         a_c.append(c)
@@ -488,7 +488,7 @@
     SB = DB // L
     KT = SEL * BANDS * P_SIZE
     dma = pltpu.SemaphoreType.DMA
-    parts = 3 if ROWS % 48 == 0 else 1
+    parts = 1
     hbm = pl.BlockSpec(memory_space=pltpu.HBM)
     vmem = pl.BlockSpec(memory_space=pltpu.VMEM)
     energy, gout, grad_weight = pl.pallas_call(

time: 32.8 us -> 32.8 us (level)
  no operation moved by 1% of the time
where the time goes in v4:
time: 32.8 us; the launch traced here: 32.6 us
  Pallas kernels  32 us (98%)
  between operations  0.64 us (2%)
    pallas_call x1, Pallas kernels, shards(): pl.pallas_call(functools.partial(body, G, L, LM, BANDS, COLS), out_shape=...  29.7 us
    pallas_call x1, Pallas kernels, shards(): pl.pallas_call(functools.partial(finish, parts), out_shape=(jax.ShapeDtyp...  2.27 us

profile of v4, /device:TPU:0, one launch (start us, length us, event | category | flops | bytes accessed | tf_op | source)
XLA Modules:
  0.0 32.6 jit_solution(5852840336524216175)
XLA Ops:
  0.6 29.7 %shard_map.76 = (f32[1,1]{1,0:T(1,128)}, bf16[2,720,1024]{2,1,0:T(8,128)(2,1)S(1)}, f32[32,128]{1,0:T(8,128)S(1)}) custom-call(s32[8]{0:T(128)} %chan_hbm.1, s32[2]{0:T(128)} %band_hbm.1, bf16[2,720,1024]{2,1,0:T(8,128)(2,1)} %bitcast.7, bf16[83,16,1024]{2,1,0:T(8,128)(2,1)} %bitcast.8, f32[64,1440]{1,0:T(8,128)} %bitcast.9), custom_call_target="tpu_custom_call" | custom-call | tf_op jit(solution)/shard_map/pallas_call | solution.py:494
  30.4 2.3 %shard_map.77 = (f32[1,1]{1,0:T(1,128)}, bf16[2,720,1024]{2,1,0:T(8,128)(2,1)}, f32[32,128]{1,0:T(8,128)}) custom-call(f32[1,1]{1,0:T(1,128)} %get-tuple-element.9.energy_in, bf16[2,720,1024]{2,1,0:T(8,128)(2,1)S(1)} %get-tuple-element.10.gout, f32[32,128]{1,0:T(8,128)S(1)} %get-tuple-element.11.gw_in), custom_call_target="tpu_custom_call" | custom-call | tf_op jit(solution)/shard_map/pallas_call | solution.py:555
